TPU v7x, 32 devices: a whole 2x2x4 slice. The times are simulated.
32 devices in a mesh: bx: 4 (over z), by: 8 (over y, x, core).
Axes of the slice: x: 2, y: 2, z: 4, core: 2. Of those that a mesh axis runs over, the one named last changes fastest.
Arguments:
- adjoint_source: float32 [5, 16, 32, 512], P(None, 'bx', 'by'), may hold values from -5 to 5
- initial: float32 [5, 16, 32, 512], P(None, 'bx', 'by'), may hold values from -6 to 6
- inverses: float32 [5, 5, 16, 32, 512], P(None, None, 'bx', 'by'), may hold values from -0.23 to 0.48
- couplings: bfloat16 [6, 5, 5, 16, 32, 512], P(None, None, None, 'bx', 'by'), may hold values from -3.7 to 1.3
- interface_tiles: float32 [32, 5, 5, 64], P(('bx', 'by')), may hold values from -2.5 to 2.5
- source_cells: int32 [32, 64], P(('bx', 'by')), may hold values from 0 to 8191
- target_cells: int32 [32, 64], P(('bx', 'by')), may hold values from 0 to 8191
- tile_counts: int32 [32, 32], P(('bx', 'by')), may hold values from 1 to 2, as said below
Outputs:
- adjoint: float32 [5, 16, 32, 512], P(None, 'bx', 'by')
Inputs may be any that keep to these rules, and one draw needn't show every extreme that they name: Slots k of the group of receiving block d with k < tile_counts[o, d] hold tiles; the others are padding. In every draw one receiving block gets 2 tiles from every block.
All inputs are finite; a program needn't handle non-finite values.
Results may differ from a plain program's by a relative error of at most 0.0003.
Values sent between devices are 32-bit elements; how exact they have to be, the bound alone decides.
A program may use at most 64 MiB of HBM per device.

v0:
```python
import jax
import jax.numpy as jnp
from jax import lax
from jax.sharding import PartitionSpec as P

ITERS = 2


def shifted(block, axis, distance):
    devices = range(lax.axis_size(axis))
    route = [(i - distance, i) for i in devices if i - distance in devices]
    return lax.ppermute(block, axis, route)


def matvec(matrix, vector):
    return jnp.sum(matrix.astype(jnp.float32) * vector[None], axis=1)


def neighbour(values, axis_at, offset):
    length = values.shape[axis_at]
    border = jnp.zeros_like(lax.slice_in_dim(values, 0, 1, axis=axis_at))
    if offset > 0:
        return jnp.concatenate(
            [lax.slice_in_dim(values, 1, length, axis=axis_at), border], axis=axis_at
        )
    return jnp.concatenate(
        [border, lax.slice_in_dim(values, 0, length - 1, axis=axis_at)], axis=axis_at
    )


def send_faces(across_x, across_y, offset):
    return (shifted(across_x, "bx", offset), shifted(across_y, "by", offset))


def solve_block(fixed, inverses, along_x, along_y, inflow_x, inflow_y, forward):
    count_x = fixed.shape[1]
    count_y = fixed.shape[2]
    order_x = list(range(count_x)) if forward else list(reversed(range(count_x)))
    order_y = list(range(count_y)) if forward else list(reversed(range(count_y)))
    offset = -1 if forward else 1
    finished = {}
    for x in order_x:
        for y in order_y:
            from_x = finished[x + offset, y] if (x + offset, y) in finished else inflow_x[:, y]
            from_y = finished[x, y + offset] if (x, y + offset) in finished else inflow_y[:, x]
            right = (
                fixed[:, x, y]
                - matvec(along_x[:, :, x, y], from_x)
                - matvec(along_y[:, :, x, y], from_y)
            )
            finished[x, y] = matvec(inverses[:, :, x, y], right)
    planes = [jnp.stack([finished[x, y] for y in range(count_y)], axis=1) for x in range(count_x)]
    return jnp.stack(planes, axis=1)


def wavefront(fixed, inverses, along_x, along_y, forward, pieces):
    count_x = fixed.shape[1]
    count_y = fixed.shape[2]
    width = fixed.shape[3] // pieces
    offset = 1 if forward else -1
    if forward:
        my_turn = lax.axis_index("bx") + lax.axis_index("by")
    else:
        my_turn = (
            lax.axis_size("bx")
            - 1
            - lax.axis_index("bx")
            + (lax.axis_size("by") - 1 - lax.axis_index("by"))
        )
    total = lax.axis_size("bx") + lax.axis_size("by") - 2 + pieces
    edge_x = count_x - 1 if forward else 0
    edge_y = count_y - 1 if forward else 0
    start_x = jnp.zeros((fixed.shape[0], count_y, width), jnp.float32)
    start_y = jnp.zeros((fixed.shape[0], count_x, width), jnp.float32)

    def advance(t, carry):
        result, out_x, out_y = carry
        inflow_x, inflow_y = send_faces(out_x, out_y, offset)
        piece = t - my_turn

        def active():
            first = jnp.clip(piece, 0, pieces - 1).astype(jnp.int32) * width

            def slab_of(source):
                return lax.dynamic_slice_in_dim(source, first, width, axis=source.ndim - 1)

            block = solve_block(
                slab_of(fixed),
                slab_of(inverses),
                slab_of(along_x),
                slab_of(along_y),
                inflow_x,
                inflow_y,
                forward,
            )
            return (
                lax.dynamic_update_slice_in_dim(result, block, first, axis=3),
                block[:, edge_x],
                block[:, :, edge_y],
            )

        def resting():
            return (result, out_x, out_y)

        return lax.cond((piece >= 0) & (piece < pieces), active, resting)

    result, out_x, out_y = lax.fori_loop(
        0, total, advance, (jnp.zeros_like(fixed), start_x, start_y)
    )
    return result


def interface(iterate, interface_tiles, source_cells, target_cells, tile_counts):
    var_count = iterate.shape[0]
    flat_cells = iterate.reshape(var_count, -1)
    block_count = lax.axis_size("bx") * lax.axis_size("by")
    slot_count = source_cells.shape[1]
    per_pair = slot_count // block_count
    picked = jnp.take(flat_cells, source_cells[0], axis=1)
    products = jnp.sum(interface_tiles[0] * picked[None], axis=1)
    slot_ids = jnp.arange(slot_count, dtype=jnp.int32)
    limits = jnp.repeat(tile_counts[0], per_pair)
    products = jnp.where((slot_ids % per_pair)[None] < limits[None], products, 0.0)
    arrived = lax.all_to_all(products, ("bx", "by"), split_axis=1, concat_axis=1, tiled=True)
    summed = jnp.zeros_like(flat_cells).at[:, target_cells[0]].add(arrived)
    return summed.reshape(iterate.shape)


def per_device(
    adjoint_source,
    initial,
    inverses,
    couplings,
    interface_tiles,
    source_cells,
    target_cells,
    tile_counts,
):
    pieces = 1
    iterate = initial
    for number in range(ITERS):
        inter = interface(iterate, interface_tiles, source_cells, target_cells, tile_counts)
        base = adjoint_source - inter
        rim_x, rim_y = send_faces(iterate[:, 0], iterate[:, :, 0], -1)
        above_x = jnp.concatenate([iterate[:, 1:], rim_x[:, None]], axis=1)
        above_y = jnp.concatenate([iterate[:, :, 1:], rim_y[:, :, None]], axis=2)
        lower_terms = (
            base
            - matvec(couplings[1], above_x)
            - matvec(couplings[3], above_y)
            - matvec(couplings[4], neighbour(iterate, 3, -1))
            - matvec(couplings[5], neighbour(iterate, 3, 1))
        )
        half = wavefront(lower_terms, inverses, couplings[0], couplings[2], True, pieces)
        rim_x, rim_y = send_faces(half[:, -1], half[:, :, -1], 1)
        below_x = jnp.concatenate([rim_x[:, None], half[:, :-1]], axis=1)
        below_y = jnp.concatenate([rim_y[:, :, None], half[:, :, :-1]], axis=2)
        upper_terms = (
            base
            - matvec(couplings[0], below_x)
            - matvec(couplings[2], below_y)
            - matvec(couplings[4], neighbour(half, 3, -1))
            - matvec(couplings[5], neighbour(half, 3, 1))
        )
        iterate = wavefront(upper_terms, inverses, couplings[1], couplings[3], False, pieces)
    return iterate


def solution(mesh):
    return jax.shard_map(
        per_device,
        mesh=mesh,
        in_specs=(
            P(None, "bx", "by", None),
            P(None, "bx", "by", None),
            P(None, None, "bx", "by", None),
            P(None, None, None, "bx", "by", None),
            P(("bx", "by"), None, None, None),
            P(("bx", "by"), None),
            P(("bx", "by"), None),
            P(("bx", "by"), None),
        ),
        out_specs=P(None, "bx", "by", None),
        check_vma=False,
    )
```

profile of v0, /device:TPU:0, one launch (start us, length us, event | category | flops | bytes accessed | tf_op | source)
XLA Modules:
  0.0 592.0 jit_solution(7805730527410884980)
XLA Ops:
  9.8 8.6 %all-to-all-start = ((f32[5,32,2]{0,2,1:T(2,128)}), f32[5,32,2]{0,2,1:T(2,128)S(1)}, u32[]{:S(2)}, u32[]{:S(2)}) async-start(f32[5,32,2]{0,2,1:T(2,128)} %broadcast_select_fusion.1), calls=%async_computation | async-start | bytes 65536 | tf_op jit(solution)/shard_map/all_to_all | solution.py:124
  38.6 109.1 %while.68 = (s32[]{:T(128)}, f32[5,4,4,512]{3,0,2,1:T(8,128)}, f32[5,4,512]{2,0,1:T(8,128)}, f32[5,4,512]{2,0,1:T(8,128)}, s32[]{:T(128)}, /*index=5*/f32[5,5,4,...) while((s32[]{:T(128)}, f32[5,4,4,512]{3,0,2,1:T(8,128)}, ...), condition=%wide.region_57.59_spmd, body=%wide.region_6.58_spmd.sunk | while | flops 1873927 | bytes 7762251 | solution.py:107
  45.8 6.1 %conditional.8 = ((f32[5,4,4,512]{3,0,2,1:T(8,128)}, f32[5,4,512]{2,0,1:T(8,128)}, f32[5,4,512]{2,0,1:T(8,128)})) conditional(s32[]{:T(128)} %convert_element_type.1152, (f32[5,4,4,512]{3,0,2,1:T(8,128)}, f32[5,4,512]{2,0,1:T(8,128)}, f32[5,4,512]{2,0,1:T(8,128)}) %tuple.341, (f32[5,5,4,4,512]{4,3,2,1,0:T(4,128)S(1)}, ...), branch_computations={%region_7.8_spmd, %region_8.57_spmd} | conditional | flops 1873920 | bytes 7434272 | solution.py:105
  55.5 10.0 %collective-permute-start = (f32[5,4,512]{2,0,1:T(8,128)}, f32[5,4,512]{2,0,1:T(8,128)S(1)}, u32[]{:S(2)}, u32[]{:S(2)}) collective-permute-start(f32[5,4,512]{2,0,1:T(8,128)} %get-tuple-element.1513), channel_id=1, source_target_pairs={{0,8},{8,16},{16,24},{1,9},{9,17},{17,25},{2,10},{10,18},{18,26},{... | collective-permute-start | bytes 122888 | tf_op jit(solution)/shard_map/while/body/eval_jaxpr/ppermute | solution.py:12
  71.9 6.3 %collective-permute-start.1 = (f32[5,4,512]{2,0,1:T(8,128)}, f32[5,4,512]{2,0,1:T(8,128)S(1)}, u32[]{:S(2)}, u32[]{:S(2)}) collective-permute-start(f32[5,4,512]{2,0,1:T(8,128)} %get-tuple-element.1514), channel_id=1, source_target_pairs={{0,1},{1,2},{2,3},{3,4},{4,5},{5,6},{6,7},{8,9},{9,10},{10,11},{11... | collective-permute-start | bytes 122888 | tf_op jit(solution)/shard_map/while/body/eval_jaxpr/ppermute | solution.py:12
  86.0 7.3 %collective-permute-start = (f32[5,4,512]{2,0,1:T(8,128)}, f32[5,4,512]{2,0,1:T(8,128)S(1)}, u32[]{:S(2)}, u32[]{:S(2)}) collective-permute-start(f32[5,4,512]{2,0,1:T(8,128)} %get-tuple-element.1513), channel_id=1, source_target_pairs={{0,8},{8,16},{16,24},{1,9},{9,17},{17,25},{2,10},{10,18},{18,26},{... | collective-permute-start | bytes 122888 | tf_op jit(solution)/shard_map/while/body/eval_jaxpr/ppermute | solution.py:12
  101.0 9.1 %collective-permute-start.1 = (f32[5,4,512]{2,0,1:T(8,128)}, f32[5,4,512]{2,0,1:T(8,128)S(1)}, u32[]{:S(2)}, u32[]{:S(2)}) collective-permute-start(f32[5,4,512]{2,0,1:T(8,128)} %get-tuple-element.1514), channel_id=1, source_target_pairs={{0,1},{1,2},{2,3},{3,4},{4,5},{5,6},{6,7},{8,9},{9,10},{10,11},{11... | collective-permute-start | bytes 122888 | tf_op jit(solution)/shard_map/while/body/eval_jaxpr/ppermute | solution.py:12
  118.9 6.6 %collective-permute-start = (f32[5,4,512]{2,0,1:T(8,128)}, f32[5,4,512]{2,0,1:T(8,128)S(1)}, u32[]{:S(2)}, u32[]{:S(2)}) collective-permute-start(f32[5,4,512]{2,0,1:T(8,128)} %get-tuple-element.1513), channel_id=1, source_target_pairs={{0,8},{8,16},{16,24},{1,9},{9,17},{17,25},{2,10},{10,18},{18,26},{... | collective-permute-start | bytes 122888 | tf_op jit(solution)/shard_map/while/body/eval_jaxpr/ppermute | solution.py:12
  155.0 9.3 %collective-permute-start.11 = (f32[5,4,512]{2,0,1:T(8,128)S(1)}, f32[5,4,512]{2,0,1:T(8,128)S(1)}, u32[]{:S(2)}, u32[]{:S(2)}) collective-permute-start(f32[5,4,512]{2,0,1:T(8,128)S(1)} %slice_bitcast_fusion.75), channel_id=1, source_target_pairs={{0,1},{1,2},{2,3},{3,4},{4,5},{5,6},{6,7},{8,9},{9,10},{10,11},{11... | collective-permute-start | bytes 122888 | tf_op jit(solution)/shard_map/ppermute | solution.py:12
  167.5 128.4 %while.69 = (s32[]{:T(128)}, f32[5,4,4,512]{3,0,2,1:T(8,128)}, f32[5,4,512]{2,0,1:T(8,128)S(1)}, f32[5,4,512]{2,0,1:T(8,128)S(1)}, s32[]{:T(128)}, /*index=5*/f3...) while((s32[]{:T(128)}, f32[5,4,4,512]{3,0,2,1:T(8,128)}, ...), condition=%wide.region_113.115_spmd, body=%wide.region_62.114_spmd.sunk | while | flops 1873927 | bytes 7762251 | solution.py:107
  202.3 6.1 %collective-permute-done.2 = f32[5,4,512]{2,0,1:T(8,128)S(1)} collective-permute-done((f32[5,4,512]{2,0,1:T(8,128)S(1)}, f32[5,4,512]{2,0,1:T(8,128)S(1)}, u32[]{:S(2)}, u32[]{:S(2)}) %collective-permute-start.2) | collective-permute-done | bytes 40992 | tf_op jit(solution)/shard_map/while/body/eval_jaxpr/ppermute | solution.py:12
  227.7 5.8 collective-permute-done.2
  244.5 5.8 collective-permute-done.2
  252.9 38.2 %collective-permute-done.2 = f32[5,4,512]{2,0,1:T(8,128)S(1)} collective-permute-done((f32[5,4,512]{2,0,1:T(8,128)S(1)}, f32[5,4,512]{2,0,1:T(8,128)S(1)}, u32[]{:S(2)}, u32[]{:S(2)}) %collective-permute-start.2) | collective-permute-done | bytes 40992 | tf_op jit(solution)/shard_map/while/body/eval_jaxpr/ppermute | solution.py:12
  332.7 109.9 %while.70 = (s32[]{:T(128)}, f32[5,4,4,512]{3,0,2,1:T(8,128)}, f32[5,4,512]{2,0,1:T(8,128)}, f32[5,4,512]{2,0,1:T(8,128)}, s32[]{:T(128)}, /*index=5*/f32[5,5,4,...) while((s32[]{:T(128)}, f32[5,4,4,512]{3,0,2,1:T(8,128)}, ...), condition=%wide.region_171.173_spmd, body=%wide.region_120.172_spmd.sunk | while | flops 1873927 | bytes 7762251 | solution.py:107
  340.8 6.1 %conditional.10 = ((f32[5,4,4,512]{3,0,2,1:T(8,128)}, f32[5,4,512]{2,0,1:T(8,128)}, f32[5,4,512]{2,0,1:T(8,128)})) conditional(s32[]{:T(128)} %convert_element_type.1154, (f32[5,4,4,512]{3,0,2,1:T(8,128)}, f32[5,4,512]{2,0,1:T(8,128)}, f32[5,4,512]{2,0,1:T(8,128)}) %tuple.347, (f32[5,5,4,4,512]{4,3,2,1,0:T(4,128)S(1)}, ...), branch_computations={%region_121.122_spmd, %region_122.171_spmd} | conditional | flops 1873920 | bytes 7434272 | solution.py:105
  350.5 10.0 %collective-permute-start.4 = (f32[5,4,512]{2,0,1:T(8,128)}, f32[5,4,512]{2,0,1:T(8,128)S(1)}, u32[]{:S(2)}, u32[]{:S(2)}) collective-permute-start(f32[5,4,512]{2,0,1:T(8,128)} %get-tuple-element.1579), channel_id=1, source_target_pairs={{0,8},{8,16},{16,24},{1,9},{9,17},{17,25},{2,10},{10,18},{18,26},{... | collective-permute-start | bytes 122888 | tf_op jit(solution)/shard_map/while/body/eval_jaxpr/ppermute | solution.py:12
  366.9 6.3 %collective-permute-start.5 = (f32[5,4,512]{2,0,1:T(8,128)}, f32[5,4,512]{2,0,1:T(8,128)S(1)}, u32[]{:S(2)}, u32[]{:S(2)}) collective-permute-start(f32[5,4,512]{2,0,1:T(8,128)} %get-tuple-element.1580), channel_id=1, source_target_pairs={{0,1},{1,2},{2,3},{3,4},{4,5},{5,6},{6,7},{8,9},{9,10},{10,11},{11... | collective-permute-start | bytes 122888 | tf_op jit(solution)/shard_map/while/body/eval_jaxpr/ppermute | solution.py:12
  381.0 7.3 %collective-permute-start.4 = (f32[5,4,512]{2,0,1:T(8,128)}, f32[5,4,512]{2,0,1:T(8,128)S(1)}, u32[]{:S(2)}, u32[]{:S(2)}) collective-permute-start(f32[5,4,512]{2,0,1:T(8,128)} %get-tuple-element.1579), channel_id=1, source_target_pairs={{0,8},{8,16},{16,24},{1,9},{9,17},{17,25},{2,10},{10,18},{18,26},{... | collective-permute-start | bytes 122888 | tf_op jit(solution)/shard_map/while/body/eval_jaxpr/ppermute | solution.py:12
  396.0 9.1 %collective-permute-start.5 = (f32[5,4,512]{2,0,1:T(8,128)}, f32[5,4,512]{2,0,1:T(8,128)S(1)}, u32[]{:S(2)}, u32[]{:S(2)}) collective-permute-start(f32[5,4,512]{2,0,1:T(8,128)} %get-tuple-element.1580), channel_id=1, source_target_pairs={{0,1},{1,2},{2,3},{3,4},{4,5},{5,6},{6,7},{8,9},{9,10},{10,11},{11... | collective-permute-start | bytes 122888 | tf_op jit(solution)/shard_map/while/body/eval_jaxpr/ppermute | solution.py:12
  413.9 6.6 %collective-permute-start.4 = (f32[5,4,512]{2,0,1:T(8,128)}, f32[5,4,512]{2,0,1:T(8,128)S(1)}, u32[]{:S(2)}, u32[]{:S(2)}) collective-permute-start(f32[5,4,512]{2,0,1:T(8,128)} %get-tuple-element.1579), channel_id=1, source_target_pairs={{0,8},{8,16},{16,24},{1,9},{9,17},{17,25},{2,10},{10,18},{18,26},{... | collective-permute-start | bytes 122888 | tf_op jit(solution)/shard_map/while/body/eval_jaxpr/ppermute | solution.py:12
  444.7 9.5 %collective-permute-start.15 = (f32[5,4,512]{2,0,1:T(8,128)S(1)}, f32[5,4,512]{2,0,1:T(8,128)S(1)}, u32[]{:S(2)}, u32[]{:S(2)}) collective-permute-start(f32[5,4,512]{2,0,1:T(8,128)S(1)} %slice_bitcast_fusion.74), channel_id=1, source_target_pairs={{0,1},{1,2},{2,3},{3,4},{4,5},{5,6},{6,7},{8,9},{9,10},{10,11},{11... | collective-permute-start | bytes 122888 | tf_op jit(solution)/shard_map/ppermute | solution.py:12
  463.2 127.1 %while.71 = (s32[]{:T(128)}, f32[5,4,4,512]{3,0,2,1:T(8,128)}, f32[5,4,512]{2,0,1:T(8,128)S(1)}, f32[5,4,512]{2,0,1:T(8,128)S(1)}, s32[]{:T(128)}, /*index=5*/f3...) while((s32[]{:T(128)}, f32[5,4,4,512]{3,0,2,1:T(8,128)}, ...), condition=%wide.region_227.229_spmd, body=%wide.region_176.228_spmd.sunk | while | flops 1873927 | bytes 7762251 | solution.py:107
  547.4 38.1 %collective-permute-done.6 = f32[5,4,512]{2,0,1:T(8,128)S(1)} collective-permute-done((f32[5,4,512]{2,0,1:T(8,128)S(1)}, f32[5,4,512]{2,0,1:T(8,128)S(1)}, u32[]{:S(2)}, u32[]{:S(2)}) %collective-permute-start.6) | collective-permute-done | bytes 40992 | tf_op jit(solution)/shard_map/while/body/eval_jaxpr/ppermute | solution.py:12
  (625 shorter events, 397.8 us)
Async XLA Ops:
  1.0 31.2 %collective-permute-start.9 = (f32[5,4,512]{2,1,0:T(4,128)S(1)}, f32[5,4,512]{2,1,0:T(4,128)}, u32[]{:S(2)}, u32[]{:S(2)}) collective-permute-start(f32[5,4,512]{2,1,0:T(4,128)S(1)} %bitcast.1360), channel_id=1, source_target_pairs={{1,0},{2,1},{3,2},{4,3},{5,4},{6,5},{7,6},{9,8},{10,9},{11,10},{12... | collective-permute-start | bytes 122888 | tf_op jit(solution)/shard_map/ppermute | solution.py:12
  9.8 15.9 %all-to-all-start = ((f32[5,32,2]{0,2,1:T(2,128)}), f32[5,32,2]{0,2,1:T(2,128)S(1)}, u32[]{:S(2)}, u32[]{:S(2)}) async-start(f32[5,32,2]{0,2,1:T(2,128)} %broadcast_select_fusion.1), calls=%async_computation | async-start | bytes 65536 | tf_op jit(solution)/shard_map/all_to_all | solution.py:124
  19.0 14.9 %collective-permute-start.8 = (f32[5,4,512]{2,1,0:T(4,128)}, f32[5,4,512]{2,1,0:T(4,128)S(1)}, u32[]{:S(2)}, u32[]{:S(2)}) collective-permute-start(f32[5,4,512]{2,1,0:T(4,128)} %slice_bitcast_fusion.80), channel_id=1, source_target_pairs={{8,0},{16,8},{24,16},{9,1},{17,9},{25,17},{10,2},{18,10},{26,18},{... | collective-permute-start | bytes 122888 | tf_op jit(solution)/shard_map/ppermute | solution.py:12
  55.5 12.2 %collective-permute-start = (f32[5,4,512]{2,0,1:T(8,128)}, f32[5,4,512]{2,0,1:T(8,128)S(1)}, u32[]{:S(2)}, u32[]{:S(2)}) collective-permute-start(f32[5,4,512]{2,0,1:T(8,128)} %get-tuple-element.1513), channel_id=1, source_target_pairs={{0,8},{8,16},{16,24},{1,9},{9,17},{17,25},{2,10},{10,18},{18,26},{... | collective-permute-start | bytes 122888 | tf_op jit(solution)/shard_map/while/body/eval_jaxpr/ppermute | solution.py:12
  68.1 10.2 %collective-permute-start = (f32[5,4,512]{2,0,1:T(8,128)}, f32[5,4,512]{2,0,1:T(8,128)S(1)}, u32[]{:S(2)}, u32[]{:S(2)}) collective-permute-start(f32[5,4,512]{2,0,1:T(8,128)} %get-tuple-element.1513), channel_id=1, source_target_pairs={{0,8},{8,16},{16,24},{1,9},{9,17},{17,25},{2,10},{10,18},{18,26},{... | collective-permute-start | bytes 122888 | tf_op jit(solution)/shard_map/while/body/eval_jaxpr/ppermute | solution.py:12
  86.0 11.7 %collective-permute-start = (f32[5,4,512]{2,0,1:T(8,128)}, f32[5,4,512]{2,0,1:T(8,128)S(1)}, u32[]{:S(2)}, u32[]{:S(2)}) collective-permute-start(f32[5,4,512]{2,0,1:T(8,128)} %get-tuple-element.1513), channel_id=1, source_target_pairs={{0,8},{8,16},{16,24},{1,9},{9,17},{17,25},{2,10},{10,18},{18,26},{... | collective-permute-start | bytes 122888 | tf_op jit(solution)/shard_map/while/body/eval_jaxpr/ppermute | solution.py:12
  98.8 11.3 %collective-permute-start = (f32[5,4,512]{2,0,1:T(8,128)}, f32[5,4,512]{2,0,1:T(8,128)S(1)}, u32[]{:S(2)}, u32[]{:S(2)}) collective-permute-start(f32[5,4,512]{2,0,1:T(8,128)} %get-tuple-element.1513), channel_id=1, source_target_pairs={{0,8},{8,16},{16,24},{1,9},{9,17},{17,25},{2,10},{10,18},{18,26},{... | collective-permute-start | bytes 122888 | tf_op jit(solution)/shard_map/while/body/eval_jaxpr/ppermute | solution.py:12
  101.0 10.2 %collective-permute-start.1 = (f32[5,4,512]{2,0,1:T(8,128)}, f32[5,4,512]{2,0,1:T(8,128)S(1)}, u32[]{:S(2)}, u32[]{:S(2)}) collective-permute-start(f32[5,4,512]{2,0,1:T(8,128)} %get-tuple-element.1514), channel_id=1, source_target_pairs={{0,1},{1,2},{2,3},{3,4},{4,5},{5,6},{6,7},{8,9},{9,10},{10,11},{11... | collective-permute-start | bytes 122888 | tf_op jit(solution)/shard_map/while/body/eval_jaxpr/ppermute | solution.py:12
  118.9 11.3 %collective-permute-start = (f32[5,4,512]{2,0,1:T(8,128)}, f32[5,4,512]{2,0,1:T(8,128)S(1)}, u32[]{:S(2)}, u32[]{:S(2)}) collective-permute-start(f32[5,4,512]{2,0,1:T(8,128)} %get-tuple-element.1513), channel_id=1, source_target_pairs={{0,8},{8,16},{16,24},{1,9},{9,17},{17,25},{2,10},{10,18},{18,26},{... | collective-permute-start | bytes 122888 | tf_op jit(solution)/shard_map/while/body/eval_jaxpr/ppermute | solution.py:12
  149.7 14.8 %collective-permute-start.10 = (f32[5,4,512]{2,0,1:T(8,128)S(1)}, f32[5,4,512]{2,0,1:T(8,128)S(1)}, u32[]{:S(2)}, u32[]{:S(2)}) collective-permute-start(f32[5,4,512]{2,0,1:T(8,128)S(1)} %slice_bitcast_fusion.79), channel_id=1, source_target_pairs={{0,8},{8,16},{16,24},{1,9},{9,17},{17,25},{2,10},{10,18},{18,26},{... | collective-permute-start | bytes 122888 | tf_op jit(solution)/shard_map/ppermute | solution.py:12
  250.3 40.8 %collective-permute-start.2 = (f32[5,4,512]{2,0,1:T(8,128)S(1)}, f32[5,4,512]{2,0,1:T(8,128)S(1)}, u32[]{:S(2)}, u32[]{:S(2)}) collective-permute-start(f32[5,4,512]{2,0,1:T(8,128)S(1)} %get-tuple-element.1546), channel_id=1, source_target_pairs={{8,0},{16,8},{24,16},{9,1},{17,9},{25,17},{10,2},{18,10},{26,18},{... | collective-permute-start | bytes 122888 | tf_op jit(solution)/shard_map/while/body/eval_jaxpr/ppermute | solution.py:12
  251.6 39.5 %collective-permute-start.3 = (f32[5,4,512]{2,0,1:T(8,128)S(1)}, f32[5,4,512]{2,0,1:T(8,128)S(1)}, u32[]{:S(2)}, u32[]{:S(2)}) collective-permute-start(f32[5,4,512]{2,0,1:T(8,128)S(1)} %get-tuple-element.1547), channel_id=1, source_target_pairs={{1,0},{2,1},{3,2},{4,3},{5,4},{6,5},{7,6},{9,8},{10,9},{11,10},{12... | collective-permute-start | bytes 122888 | tf_op jit(solution)/shard_map/while/body/eval_jaxpr/ppermute | solution.py:12
  307.2 11.6 %all-to-all-start.1 = ((f32[5,32,2]{0,2,1:T(2,128)}), f32[5,32,2]{0,2,1:T(2,128)S(1)}, u32[]{:S(2)}, u32[]{:S(2)}) async-start(f32[5,32,2]{0,2,1:T(2,128)} %broadcast_select_fusion), calls=%async_computation.1 | async-start | bytes 65536 | tf_op jit(solution)/shard_map/all_to_all | solution.py:124
  309.8 15.7 %collective-permute-start.13 = (f32[5,4,512]{2,0,1:T(8,128)}, f32[5,4,512]{2,0,1:T(8,128)}, u32[]{:S(2)}, u32[]{:S(2)}) collective-permute-start(f32[5,4,512]{2,0,1:T(8,128)} %slice_bitcast_fusion.77), channel_id=1, source_target_pairs={{1,0},{2,1},{3,2},{4,3},{5,4},{6,5},{7,6},{9,8},{10,9},{11,10},{12... | collective-permute-start | bytes 122888 | tf_op jit(solution)/shard_map/ppermute | solution.py:12
  316.0 11.2 %collective-permute-start.12 = (f32[5,4,512]{2,0,1:T(8,128)}, f32[5,4,512]{2,0,1:T(8,128)}, u32[]{:S(2)}, u32[]{:S(2)}) collective-permute-start(f32[5,4,512]{2,0,1:T(8,128)} %slice_bitcast_fusion.78), channel_id=1, source_target_pairs={{8,0},{16,8},{24,16},{9,1},{17,9},{25,17},{10,2},{18,10},{26,18},{... | collective-permute-start | bytes 122888 | tf_op jit(solution)/shard_map/ppermute | solution.py:12
  350.5 12.2 %collective-permute-start.4 = (f32[5,4,512]{2,0,1:T(8,128)}, f32[5,4,512]{2,0,1:T(8,128)S(1)}, u32[]{:S(2)}, u32[]{:S(2)}) collective-permute-start(f32[5,4,512]{2,0,1:T(8,128)} %get-tuple-element.1579), channel_id=1, source_target_pairs={{0,8},{8,16},{16,24},{1,9},{9,17},{17,25},{2,10},{10,18},{18,26},{... | collective-permute-start | bytes 122888 | tf_op jit(solution)/shard_map/while/body/eval_jaxpr/ppermute | solution.py:12
  363.0 10.2 %collective-permute-start.4 = (f32[5,4,512]{2,0,1:T(8,128)}, f32[5,4,512]{2,0,1:T(8,128)S(1)}, u32[]{:S(2)}, u32[]{:S(2)}) collective-permute-start(f32[5,4,512]{2,0,1:T(8,128)} %get-tuple-element.1579), channel_id=1, source_target_pairs={{0,8},{8,16},{16,24},{1,9},{9,17},{17,25},{2,10},{10,18},{18,26},{... | collective-permute-start | bytes 122888 | tf_op jit(solution)/shard_map/while/body/eval_jaxpr/ppermute | solution.py:12
  381.0 11.7 %collective-permute-start.4 = (f32[5,4,512]{2,0,1:T(8,128)}, f32[5,4,512]{2,0,1:T(8,128)S(1)}, u32[]{:S(2)}, u32[]{:S(2)}) collective-permute-start(f32[5,4,512]{2,0,1:T(8,128)} %get-tuple-element.1579), channel_id=1, source_target_pairs={{0,8},{8,16},{16,24},{1,9},{9,17},{17,25},{2,10},{10,18},{18,26},{... | collective-permute-start | bytes 122888 | tf_op jit(solution)/shard_map/while/body/eval_jaxpr/ppermute | solution.py:12
  393.8 11.3 %collective-permute-start.4 = (f32[5,4,512]{2,0,1:T(8,128)}, f32[5,4,512]{2,0,1:T(8,128)S(1)}, u32[]{:S(2)}, u32[]{:S(2)}) collective-permute-start(f32[5,4,512]{2,0,1:T(8,128)} %get-tuple-element.1579), channel_id=1, source_target_pairs={{0,8},{8,16},{16,24},{1,9},{9,17},{17,25},{2,10},{10,18},{18,26},{... | collective-permute-start | bytes 122888 | tf_op jit(solution)/shard_map/while/body/eval_jaxpr/ppermute | solution.py:12
  396.0 10.2 %collective-permute-start.5 = (f32[5,4,512]{2,0,1:T(8,128)}, f32[5,4,512]{2,0,1:T(8,128)S(1)}, u32[]{:S(2)}, u32[]{:S(2)}) collective-permute-start(f32[5,4,512]{2,0,1:T(8,128)} %get-tuple-element.1580), channel_id=1, source_target_pairs={{0,1},{1,2},{2,3},{3,4},{4,5},{5,6},{6,7},{8,9},{9,10},{10,11},{11... | collective-permute-start | bytes 122888 | tf_op jit(solution)/shard_map/while/body/eval_jaxpr/ppermute | solution.py:12
  413.9 11.3 %collective-permute-start.4 = (f32[5,4,512]{2,0,1:T(8,128)}, f32[5,4,512]{2,0,1:T(8,128)S(1)}, u32[]{:S(2)}, u32[]{:S(2)}) collective-permute-start(f32[5,4,512]{2,0,1:T(8,128)} %get-tuple-element.1579), channel_id=1, source_target_pairs={{0,8},{8,16},{16,24},{1,9},{9,17},{17,25},{2,10},{10,18},{18,26},{... | collective-permute-start | bytes 122888 | tf_op jit(solution)/shard_map/while/body/eval_jaxpr/ppermute | solution.py:12
  444.7 14.9 %collective-permute-start.15 = (f32[5,4,512]{2,0,1:T(8,128)S(1)}, f32[5,4,512]{2,0,1:T(8,128)S(1)}, u32[]{:S(2)}, u32[]{:S(2)}) collective-permute-start(f32[5,4,512]{2,0,1:T(8,128)S(1)} %slice_bitcast_fusion.74), channel_id=1, source_target_pairs={{0,1},{1,2},{2,3},{3,4},{4,5},{5,6},{6,7},{8,9},{9,10},{10,11},{11... | collective-permute-start | bytes 122888 | tf_op jit(solution)/shard_map/ppermute | solution.py:12
  544.8 40.7 %collective-permute-start.6 = (f32[5,4,512]{2,0,1:T(8,128)S(1)}, f32[5,4,512]{2,0,1:T(8,128)S(1)}, u32[]{:S(2)}, u32[]{:S(2)}) collective-permute-start(f32[5,4,512]{2,0,1:T(8,128)S(1)} %get-tuple-element.1612), channel_id=1, source_target_pairs={{8,0},{16,8},{24,16},{9,1},{17,9},{25,17},{10,2},{18,10},{26,18},{... | collective-permute-start | bytes 122888 | tf_op jit(solution)/shard_map/while/body/eval_jaxpr/ppermute | solution.py:12
  546.1 39.4 %collective-permute-start.7 = (f32[5,4,512]{2,0,1:T(8,128)S(1)}, f32[5,4,512]{2,0,1:T(8,128)S(1)}, u32[]{:S(2)}, u32[]{:S(2)}) collective-permute-start(f32[5,4,512]{2,0,1:T(8,128)S(1)} %get-tuple-element.1613), channel_id=1, source_target_pairs={{1,0},{2,1},{3,2},{4,3},{5,4},{6,5},{7,6},{9,8},{10,9},{11,10},{12... | collective-permute-start | bytes 122888 | tf_op jit(solution)/shard_map/while/body/eval_jaxpr/ppermute | solution.py:12
  (100 other events, 678.4 us)
where the time goes:
time: 596 us; the launch traced here: 592 us
  starting transfers between devices  279 us (47%)
  waiting for transfers between devices  214 us (36%)
  local copies, waits for them, and re-layouts  63.4 us (11%)
  other arithmetic  32.3 us (5%)
    ppermute x96, starting transfers between devices, shifted(): return lax.ppermute(block, axis, route)  268 us
    ppermute x96, waiting for transfers between devices, shifted(): return lax.ppermute(block, axis, route)  214 us
    reduce_sum x152, other arithmetic, matvec(): return jnp.sum(matrix.astype(jnp.float32) * vector[None], axis=1)  14.5 us
  transfers between devices with their start and end apart: 98, of which 59 were waited for; matrix products, arithmetic and copies ran while one was open for 7% of the time, Pallas kernels for 0%

commit v1 on v0

v1 whole, which is shorter than its diff:
```python
import functools

import jax
import jax.numpy as jnp
from jax import lax
from jax.experimental import pallas as pl
from jax.experimental.pallas import tpu as pltpu
from jax.sharding import PartitionSpec as P

ITERS = 2
LANES = 128
MESH = pl.DeviceIdType.MESH


def split_parts(value, axis):
    high = value.astype(jnp.bfloat16)
    low = (value - high.astype(jnp.float32)).astype(jnp.bfloat16)
    return jnp.concatenate([high, low], axis=axis)


def kernel(
    sizes,
    source_ref,
    initial_ref,
    inv_ref,
    coup_ref,
    tiles_ref,
    src_cells_ref,
    dst_cells_ref,
    counts_ref,
    out_ref,
    mats,
    inv,
    field,
    fixed,
    base,
    terms,
    products,
    out_x,
    out_y,
    in_x,
    in_y,
    prod_out,
    prod_in,
    send_x,
    send_y,
    recv_x,
    recv_y,
    send_p,
    recv_p,
):
    NP, NQ, V, CX, CY, ZT, slots, pair = sizes
    N = NP * NQ
    DIAGS = CX + CY - 1
    STEP = CX * ZT
    NEXT = STEP + ZT
    PAD = 2 * STEP
    ROWS = DIAGS * STEP
    width = min(slots, LANES)
    lane_tiles = slots // width

    p = lax.axis_index("bx")
    q = lax.axis_index("by")
    me = p * NQ + q

    barrier = pltpu.get_barrier_semaphore()

    def greet(k, carry):
        other = lax.rem(me + k, N)
        pl.semaphore_signal(
            barrier,
            inc=1,
            device_id=(lax.div(other, NQ), lax.rem(other, NQ)),
            device_id_type=MESH,
        )
        return carry

    lax.fori_loop(1, N, greet, 0)

    def first_row(x, y):
        return ((x + y) * CX + x) * ZT

    def skew(load, store_ref, lead, pad):
        for x in range(CX):
            value = load(x)
            for t in range(ZT):
                store_ref[lead, pl.ds(pad + first_row(x, 0) + t, CY, stride=STEP), :] = value[
                    :, t * LANES : (t + 1) * LANES
                ]

    field[...] = jnp.zeros_like(field)
    prod_out[...] = jnp.zeros_like(prod_out)
    for v in range(V):
        skew(lambda x: initial_ref[v, x], field, v, PAD)

    for y in range(CY):
        at = PAD + first_row(0, y)
        for v in range(V):
            out_x[0, y, v] = field[v, at : at + ZT, :]
    for x in range(CX):
        at = PAD + first_row(x, 0)
        for v in range(V):
            out_y[0, x, v] = field[v, at : at + ZT, :]

    def copy_x(s, k, to):
        return pltpu.make_async_remote_copy(
            src_ref=out_x.at[s, k],
            dst_ref=in_x.at[s, k],
            send_sem=send_x.at[s, k],
            recv_sem=recv_x.at[s, k],
            device_id=(to, q),
            device_id_type=MESH,
        )

    def copy_y(s, k, to):
        return pltpu.make_async_remote_copy(
            src_ref=out_y.at[s, k],
            dst_ref=in_y.at[s, k],
            send_sem=send_y.at[s, k],
            recv_sem=recv_y.at[s, k],
            device_id=(p, to),
            device_id_type=MESH,
        )

    def copy_p(it, other):
        return pltpu.make_async_remote_copy(
            src_ref=prod_out.at[it, lax.div(other * pair, width)],
            dst_ref=prod_in.at[it, me],
            send_sem=send_p.at[it, other],
            recv_sem=recv_p.at[it, me],
            device_id=(lax.div(other, NQ), lax.rem(other, NQ)),
            device_id_type=MESH,
        )

    pl.semaphore_wait(barrier, N - 1)

    @pl.when(p > 0)
    def _():
        for y in range(CY):
            copy_x(0, y, p - 1).start()

    @pl.when(q > 0)
    def _():
        for x in range(CX):
            copy_y(0, x, q - 1).start()

    lane_of_row = lax.broadcasted_iota(jnp.int32, (LANES, slots), 0)
    row_ids = lax.broadcasted_iota(jnp.int32, (ROWS, slots), 0)

    def places(cells):
        lane = lax.rem(cells, LANES)
        tile = lax.rem(lax.div(cells, LANES), ZT)
        column = lax.div(cells, LANES * ZT)
        x = lax.div(column, CY)
        y = lax.rem(column, CY)
        return lane, ((x + y) * CX + x) * ZT + tile

    def send_products(it):
        lane, row = places(src_cells_ref[...])
        pick_lane = jnp.where(lane_of_row == lane, 1.0, 0.0).astype(jnp.bfloat16)
        pick_lane = jnp.concatenate([pick_lane, pick_lane], axis=0)
        here = row_ids == row
        values = jnp.concatenate([field[v, PAD : PAD + ROWS, :] for v in range(V)], axis=0)
        gathered = jnp.dot(
            split_parts(values, 1), pick_lane, preferred_element_type=jnp.float32
        )
        total = jnp.zeros((V, slots), jnp.float32)
        for j in range(V):
            picked = jnp.sum(
                jnp.where(here, gathered[j * ROWS : (j + 1) * ROWS], 0.0), axis=0, keepdims=True
            )
            total = total + tiles_ref[0, :, j, :] * picked
        counts = jnp.broadcast_to(counts_ref[...].astype(jnp.float32), (8, N)).astype(jnp.bfloat16)
        slot = lax.broadcasted_iota(jnp.int32, (N, slots), 1)
        block = lax.broadcasted_iota(jnp.int32, (N, slots), 0)
        spread = jnp.where(lax.div(slot, pair) == block, 1.0, 0.0).astype(jnp.bfloat16)
        limits = jnp.dot(counts, spread, preferred_element_type=jnp.float32)
        slot_ids = lax.rem(lax.broadcasted_iota(jnp.int32, (V, slots), 1), pair)
        used = slot_ids.astype(jnp.float32) < limits[:V]
        total = jnp.where(used, total, 0.0)
        for t in range(lane_tiles):
            prod_out[it, t, 0:V, 0:width] = total[:, t * width : (t + 1) * width]
        prod_in[it, me] = prod_out[it, lax.div(me * pair, width)]

        def send(k, carry):
            copy_p(it, lax.rem(me + k, N)).start()
            return carry

        lax.fori_loop(1, N, send, 0)

    lane_ids = lax.broadcasted_iota(jnp.int32, (8, LANES), 1)

    def receive_products(it):
        def wait(k, carry):
            other = lax.rem(me + k, N)
            pltpu.make_async_remote_copy(
                src_ref=prod_out.at[it, 0],
                dst_ref=prod_in.at[it, other],
                send_sem=send_p.at[it, other],
                recv_sem=recv_p.at[it, other],
                device_id=(lax.div(other, NQ), lax.rem(other, NQ)),
                device_id_type=MESH,
            ).wait_recv()
            return carry

        lax.fori_loop(1, N, wait, 0)
        mine = lax.rem(me * pair, width)
        own = (lane_ids >= mine) & (lane_ids < mine + pair)
        per_tile = width // pair
        arrived = []
        for t in range(lane_tiles):
            total = jnp.zeros((8, LANES), jnp.float32)
            for k in range(per_tile):
                part = jnp.where(own, prod_in[it, t * per_tile + k], 0.0)
                shift = lax.rem(k * pair - mine + LANES, LANES)
                total = total + pltpu.roll(part, shift, 1)
            arrived.append(total[:, :width])
        arrived = arrived[0] if lane_tiles == 1 else jnp.concatenate(arrived, axis=1)
        lane, row = places(dst_cells_ref[...])
        put_row = jnp.where(row_ids == row, 1.0, 0.0).astype(jnp.bfloat16)
        put_row = jnp.concatenate([put_row, put_row], axis=1)
        put_lane = lane_of_row == lane
        for v in range(V):
            spread = split_parts(jnp.where(put_lane, arrived[v : v + 1], 0.0), 1)
            added = lax.dot_general(
                put_row, spread, (((1,), (1,)), ((), ())), preferred_element_type=jnp.float32
            )
            base[v] = fixed[v] - added

    send_products(0)

    def skew_coup(m, carry):
        skew(lambda x: coup_ref[m, x].astype(jnp.float32), mats, m, 0)
        return carry

    def skew_inv(m, carry):
        skew(lambda x: inv_ref[m, x], inv, m, 0)
        return carry

    lax.fori_loop(0, 6 * V * V, skew_coup, 0)
    lax.fori_loop(0, V * V, skew_inv, 0)
    for v in range(V):
        skew(lambda x: source_ref[v, x], fixed, v, 0)

    def span(d):
        low = max(0, d - CY + 1)
        high = min(d, CX - 1)
        return d * STEP + low * ZT, (high - low + 1) * ZT

    def mat(m, i, j, at, rows):
        return mats[(m * V + i) * V + j, at : at + rows, :]

    def side_products(d, m_x, m_y, sign):
        at, rows = span(d)
        from_x = [
            field[j, PAD + at + sign * NEXT : PAD + at + sign * NEXT + rows, :] for j in range(V)
        ]
        from_y = [
            field[j, PAD + at + sign * STEP : PAD + at + sign * STEP + rows, :] for j in range(V)
        ]
        sums = []
        for i in range(V):
            by_y = mat(m_y, i, 0, at, rows) * from_y[0]
            by_x = mat(m_x, i, 0, at, rows) * from_x[0]
            for j in range(1, V):
                by_y += mat(m_y, i, j, at, rows) * from_y[j]
                by_x += mat(m_x, i, j, at, rows) * from_x[j]
            sums.append(by_x + by_y)
        return sums

    def make_terms(d):
        at, rows = span(d)
        lane = lax.broadcasted_iota(jnp.int32, (rows, LANES), 1)
        tile = lax.rem(lax.broadcasted_iota(jnp.int32, (rows, LANES), 0), ZT)
        down, up = [], []
        for j in range(V):
            value = field[j, PAD + at : PAD + at + rows, :]
            before = field[j, PAD + at - 1 : PAD + at - 1 + rows, :]
            after = field[j, PAD + at + 1 : PAD + at + 1 + rows, :]
            before = jnp.where(tile == 0, 0.0, before)
            after = jnp.where(tile == ZT - 1, 0.0, after)
            down.append(pltpu.roll(jnp.where(lane == LANES - 1, before, value), 1, 1))
            up.append(pltpu.roll(jnp.where(lane == 0, after, value), LANES - 1, 1))
        for i in range(V):
            total = base[i, at : at + rows, :] - products[i, at : at + rows, :]
            low = mat(4, i, 0, at, rows) * down[0]
            high = mat(5, i, 0, at, rows) * up[0]
            for j in range(1, V):
                low += mat(4, i, j, at, rows) * down[j]
                high += mat(5, i, j, at, rows) * up[j]
            terms[i, at : at + rows, :] = total - (low + high)

    def take_x(s, k, to, at):
        copy_x(s, k, to).wait_recv()
        for v in range(V):
            field[v, PAD + at : PAD + at + ZT, :] = in_x[s, k, v]

    def take_y(s, k, to, at):
        copy_y(s, k, to).wait_recv()
        for v in range(V):
            field[v, PAD + at : PAD + at + ZT, :] = in_y[s, k, v]

    def give_x(s, k, to, at):
        for v in range(V):
            out_x[s, k, v] = field[v, PAD + at : PAD + at + ZT, :]
        copy_x(s, k, to).start()

    def give_y(s, k, to, at):
        for v in range(V):
            out_y[s, k, v] = field[v, PAD + at : PAD + at + ZT, :]
        copy_y(s, k, to).start()

    has_low_x, has_high_x = p > 0, p < NP - 1
    has_low_y, has_high_y = q > 0, q < NQ - 1

    def sweep(s, forward):
        sign = -1 if forward else 1
        m_x, m_y = (0, 2) if forward else (1, 3)
        inflow_x, outflow_x = (has_low_x, has_high_x) if forward else (has_high_x, has_low_x)
        inflow_y, outflow_y = (has_low_y, has_high_y) if forward else (has_high_y, has_low_y)
        halo, edge_x, edge_y = (-1, CX - 1, CY - 1) if forward else (None, 0, 0)
        halo_x = -1 if forward else CX
        halo_y = -1 if forward else CY
        first_x = 0 if forward else CX - 1
        first_y = 0 if forward else CY - 1
        order = range(DIAGS) if forward else range(DIAGS - 1, -1, -1)
        for d in order:
            y = d - first_x
            if 0 <= y < CY:
                pl.when(inflow_x)(
                    functools.partial(take_x, s, y, p + sign, first_row(halo_x, y))
                )
            x = d - first_y
            if 0 <= x < CX:
                pl.when(inflow_y)(
                    functools.partial(take_y, s, x, q + sign, first_row(x, halo_y))
                )
            at, rows = span(d)
            sums = side_products(d, m_x, m_y, sign)
            right = []
            for i in range(V):
                products[i, at : at + rows, :] = sums[i]
                right.append(terms[i, at : at + rows, :] - sums[i])
            for i in range(V):
                fresh = inv[i * V, at : at + rows, :] * right[0]
                for j in range(1, V):
                    fresh += inv[i * V + j, at : at + rows, :] * right[j]
                field[i, PAD + at : PAD + at + rows, :] = fresh
            y = d - edge_x
            if 0 <= y < CY:
                pl.when(outflow_x)(
                    functools.partial(give_x, s, y, p - sign, first_row(edge_x, y))
                )
            x = d - edge_y
            if 0 <= x < CX:
                pl.when(outflow_y)(
                    functools.partial(give_y, s, x, q - sign, first_row(x, edge_y))
                )

    @pl.when(has_high_x)
    def _():
        for y in range(CY):
            take_x(0, y, p + 1, first_row(CX, y))

    @pl.when(has_high_y)
    def _():
        for x in range(CX):
            take_y(0, x, q + 1, first_row(x, CY))

    for d in range(DIAGS):
        at, rows = span(d)
        sums = side_products(d, 1, 3, 1)
        for i in range(V):
            products[i, at : at + rows, :] = sums[i]

    def iteration(it, carry):
        @pl.when(it > 0)
        def _():
            send_products(it)

        receive_products(it)
        for d in range(DIAGS):
            make_terms(d)
        sweep(2 * it + 1, True)
        for d in range(DIAGS):
            make_terms(d)
        sweep(2 * it + 2, False)
        return carry

    lax.fori_loop(0, ITERS, iteration, 0)

    for v in range(V):
        for x in range(CX):
            for t in range(ZT):
                out_ref[v, x, :, t * LANES : (t + 1) * LANES] = field[
                    v, pl.ds(PAD + first_row(x, 0) + t, CY, stride=STEP), :
                ]

    def sent(k, carry):
        other = lax.rem(me + k, N)
        for it in range(ITERS):
            copy_p(it, other).wait_send()
        return carry

    lax.fori_loop(1, N, sent, 0)
    for s in range(2 * ITERS + 1):
        up = s % 2 == 1

        @pl.when(has_high_x if up else has_low_x)
        def _():
            for y in range(CY):
                copy_x(s, y, p + 1 if up else p - 1).wait_send()

        @pl.when(has_high_y if up else has_low_y)
        def _():
            for x in range(CX):
                copy_y(s, x, q + 1 if up else q - 1).wait_send()


def per_device(
    sizes_of_mesh,
    adjoint_source,
    initial,
    inverses,
    couplings,
    interface_tiles,
    source_cells,
    target_cells,
    tile_counts,
):
    NP, NQ = sizes_of_mesh
    V, CX, CY, CZ = initial.shape
    N = NP * NQ
    slots = source_cells.shape[1]
    ZT = CZ // LANES
    sizes = (NP, NQ, V, CX, CY, ZT, slots, slots // N)
    width = min(slots, LANES)
    step = CX * ZT
    rows = (CX + CY - 1) * step
    padded = rows + 4 * step
    sweeps = 2 * ITERS + 1
    vmem = pl.BlockSpec(memory_space=pltpu.VMEM)
    f32 = jnp.float32
    return pl.pallas_call(
        functools.partial(kernel, sizes),
        out_shape=jax.ShapeDtypeStruct(initial.shape, f32),
        in_specs=[vmem] * 8,
        out_specs=vmem,
        scratch_shapes=[
            pltpu.VMEM((6 * V * V, rows, LANES), f32),
            pltpu.VMEM((V * V, rows, LANES), f32),
            pltpu.VMEM((V, padded, LANES), f32),
            pltpu.VMEM((V, rows, LANES), f32),
            pltpu.VMEM((V, rows, LANES), f32),
            pltpu.VMEM((V, rows, LANES), f32),
            pltpu.VMEM((V, rows, LANES), f32),
            pltpu.VMEM((sweeps, CY, V, ZT, LANES), f32),
            pltpu.VMEM((sweeps, CX, V, ZT, LANES), f32),
            pltpu.VMEM((sweeps, CY, V, ZT, LANES), f32),
            pltpu.VMEM((sweeps, CX, V, ZT, LANES), f32),
            pltpu.VMEM((ITERS, slots // width, 8, LANES), f32),
            pltpu.VMEM((ITERS, N, 8, LANES), f32),
            pltpu.SemaphoreType.DMA((sweeps, CY)),
            pltpu.SemaphoreType.DMA((sweeps, CX)),
            pltpu.SemaphoreType.DMA((sweeps, CY)),
            pltpu.SemaphoreType.DMA((sweeps, CX)),
            pltpu.SemaphoreType.DMA((ITERS, N)),
            pltpu.SemaphoreType.DMA((ITERS, N)),
        ],
        compiler_params=pltpu.CompilerParams(
            collective_id=0, has_side_effects=True, vmem_limit_bytes=48 * 1024 * 1024
        ),
    )(
        adjoint_source,
        initial,
        inverses.reshape(V * V, CX, CY, CZ),
        couplings.reshape(6 * V * V, CX, CY, CZ),
        interface_tiles,
        source_cells,
        target_cells,
        tile_counts,
    )


def solution(mesh):
    return jax.shard_map(
        functools.partial(per_device, (mesh.shape["bx"], mesh.shape["by"])),
        mesh=mesh,
        in_specs=(
            P(None, "bx", "by", None),
            P(None, "bx", "by", None),
            P(None, None, "bx", "by", None),
            P(None, None, None, "bx", "by", None),
            P(("bx", "by"), None, None, None),
            P(("bx", "by"), None),
            P(("bx", "by"), None),
            P(("bx", "by"), None),
        ),
        out_specs=P(None, "bx", "by", None),
        check_vma=False,
    )
```

time: 596 us -> 114 us (0.19)
  starting transfers between devices: 279 us -> 0 us
  waiting for transfers between devices: 214 us -> 0 us
  Pallas kernels: 0 us -> 106 us
  local copies, waits for them, and re-layouts: 63.4 us -> 8.01 us
  other arithmetic: 32.3 us -> 0 us
    ppermute x96 -> x0, starting transfers between devices: 268 us -> none  [shifted(): return lax.ppermute(block, axis, route)]
    ppermute x96 -> x0, waiting for transfers between devices: 214 us -> none  [shifted(): return lax.ppermute(block, axis, route)]
    pallas_call x0 -> x1, Pallas kernels: none -> 106 us  [per_device(): pl.pallas_call(functools.partial(kernel, sizes), out_shape=jax.ShapeDtype...]
    slice x18 -> x0, local copies, waits for them, and re-layouts: 15.5 us -> none  [the longest x4 4.36 us: neighbour(): lax.slice_in_dim(values, 1, length, axis=axis_at)]
    reduce_sum x154 -> x0, other arithmetic: 14.5 us -> none  [the longest x152 14.5 us: matvec(): return jnp.sum(matrix.astype(jnp.float32) * vector[None], axis=1)]
    squeeze x13 -> x0, local copies, waits for them, and re-layouts: 14.2 us -> none  [the longest x4 4.61 us: active(): block[:, :, edge_y]]
    all_to_all x2 -> x0, starting transfers between devices: 11.2 us -> none  [interface(): lax.all_to_all(products, ('bx', 'by'), split_axis=1, concat_axis=1, tiled...]
    reshape x2 -> x0, local copies, waits for them, and re-layouts: 7.09 us -> none  [interface(): return summed.reshape(iterate.shape)]
  transfers between devices with their start and end apart: 98 -> 0, of which waited for: 59 -> 0; matrix products, arithmetic and copies ran while one was open for 7% -> 0% of each run, Pallas kernels for 0% -> 0%
where the time goes in v1:
time: 114 us
  Pallas kernels  106 us (93%)
  local copies, waits for them, and re-layouts  8.01 us (7%)
    pallas_call x1, Pallas kernels, per_device(): pl.pallas_call(functools.partial(kernel, sizes), out_shape=jax.ShapeDtype...  106 us
    unnamed x16, local copies, waits for them, and re-layouts  8.01 us

profile of v1, /device:TPU:0, one launch (start us, length us, event | category | flops | bytes accessed | tf_op | source)
XLA Modules:
  0.0 113.7 jit_solution(17051045704243871605)
XLA Ops:
  0.0 0.7 copy.9.tiles_ref
  0.7 0.0 copy-start
  0.7 1.7 %copy-done = bf16[6,5,5,4,4,512]{5,4,3,2,1,0:T(4,128)(2,1)S(1)} copy-done((bf16[6,5,5,4,4,512]{5,4,3,2,1,0:T(4,128)(2,1)S(1)}, bf16[6,5,5,4,4,512]{5,4,3,2,1,0:T(4,128)(2,1)}, u32[]{:S(2)}) %copy-start) | copy-done | bytes 2457624
  2.4 0.0 copy-start.1
  2.4 1.1 %copy-done.1 = f32[5,5,4,4,512]{4,3,2,1,0:T(4,128)S(1)} copy-done((f32[5,5,4,4,512]{4,3,2,1,0:T(4,128)S(1)}, f32[5,5,4,4,512]{4,3,2,1,0:T(4,128)}, u32[]{:S(2)}) %copy-start.1) | copy-done | bytes 819224
  3.5 0.0 copy-start.2
  3.6 0.9 copy-done.2
  4.5 0.0 copy-start.3
  4.5 0.9 copy-done.3
  5.4 0.0 copy-start.4
  5.4 0.7 copy-done.4
  6.0 0.0 copy-start.5
  6.0 0.7 copy-done.5
  6.7 0.0 copy-start.6
  6.7 0.7 copy-done.6
  7.3 105.7 %shard_map.82 = f32[5,4,4,512]{3,2,1,0:T(4,128)S(1)} custom-call(f32[5,4,4,512]{3,2,1,0:T(4,128)S(1)} %copy-done.2, f32[5,4,4,512]{3,2,1,0:T(4,128)S(1)} %copy-done.3, f32[25,4,4,512]{3,2,1,0:T(4,128)S(1)} %bitcast.3, bf16[150,4,4,512]{3,2,1,0:T(4,128)(2,1)S(1)} %bitcast.2, f32[1,5,5,64]{3,2,1,0:T(8,128)S(1)} %copy.9.tiles_ref, s32[1,64]{1,0:T(1,128)S(1)} %copy-done.4, ...), custom_call_target="tpu_custom_call" | custom-call | tf_op jit(solution)/shard_map/pallas_call | solution.py:444
  113.0 0.7 copy.11
Async XLA Ops:
  0.7 1.7 %copy-start = (bf16[6,5,5,4,4,512]{5,4,3,2,1,0:T(4,128)(2,1)S(1)}, bf16[6,5,5,4,4,512]{5,4,3,2,1,0:T(4,128)(2,1)}, u32[]{:S(2)}) copy-start(bf16[6,5,5,4,4,512]{5,4,3,2,1,0:T(4,128)(2,1)} %param.11) | copy-start | bytes 7372804
  2.4 1.1 %copy-start.1 = (f32[5,5,4,4,512]{4,3,2,1,0:T(4,128)S(1)}, f32[5,5,4,4,512]{4,3,2,1,0:T(4,128)}, u32[]{:S(2)}) copy-start(f32[5,5,4,4,512]{4,3,2,1,0:T(4,128)} %param.10) | copy-start | bytes 2457604
  3.5 0.9 copy-start.2
  4.5 0.9 copy-start.3
  5.4 0.7 copy-start.4
  6.0 0.7 copy-start.5
  6.7 0.7 copy-start.6

commit v2 on v1

--- a/solution.py
+++ b/solution.py
@@ -20,35 +20,33 @@
 
 def kernel(
     sizes,
-    source_ref,
-    initial_ref,
-    inv_ref,
-    coup_ref,
-    tiles_ref,
-    src_cells_ref,
-    dst_cells_ref,
-    counts_ref,
-    out_ref,
-    mats,
-    inv,
-    field,
-    fixed,
-    base,
-    terms,
-    products,
-    out_x,
-    out_y,
-    in_x,
-    in_y,
-    prod_out,
-    prod_in,
-    send_x,
-    send_y,
-    recv_x,
-    recv_y,
-    send_p,
-    recv_p,
+    *refs,
 ):
+    inputs, out_ref = refs[:8], refs[8]
+    staged, copied = refs[9:17], refs[17]
+    source_ref, initial_ref, inv_ref, coup_ref = staged[:4]
+    tiles_ref, src_cells_ref, dst_cells_ref, counts_ref = staged[4:]
+    (
+        mats,
+        inv,
+        field,
+        fixed,
+        base,
+        terms,
+        products,
+        out_x,
+        out_y,
+        in_x,
+        in_y,
+        prod_out,
+        prod_in,
+        send_x,
+        send_y,
+        recv_x,
+        recv_y,
+        send_p,
+        recv_p,
+    ) = refs[18:]
     NP, NQ, V, CX, CY, ZT, slots, pair = sizes
     N = NP * NQ
     DIAGS = CX + CY - 1
@@ -59,6 +57,12 @@
     width = min(slots, LANES)
     lane_tiles = slots // width
 
+    fetches = [
+        pltpu.make_async_copy(inputs[k], staged[k], copied.at[k]) for k in range(len(inputs))
+    ]
+    for k in (1, 4, 5, 7, 3, 2, 0, 6):
+        fetches[k].start()
+
     p = lax.axis_index("bx")
     q = lax.axis_index("by")
     me = p * NQ + q
@@ -90,6 +94,7 @@
 
     field[...] = jnp.zeros_like(field)
     prod_out[...] = jnp.zeros_like(prod_out)
+    fetches[1].wait()
     for v in range(V):
         skew(lambda x: initial_ref[v, x], field, v, PAD)
 
@@ -164,22 +169,23 @@
         gathered = jnp.dot(
             split_parts(values, 1), pick_lane, preferred_element_type=jnp.float32
         )
-        total = jnp.zeros((V, slots), jnp.float32)
+        totals = [jnp.zeros((1, slots), jnp.float32)] * V
         for j in range(V):
             picked = jnp.sum(
                 jnp.where(here, gathered[j * ROWS : (j + 1) * ROWS], 0.0), axis=0, keepdims=True
             )
-            total = total + tiles_ref[0, :, j, :] * picked
+            totals = [totals[i] + tiles_ref[i, j] * picked for i in range(V)]
         counts = jnp.broadcast_to(counts_ref[...].astype(jnp.float32), (8, N)).astype(jnp.bfloat16)
         slot = lax.broadcasted_iota(jnp.int32, (N, slots), 1)
         block = lax.broadcasted_iota(jnp.int32, (N, slots), 0)
         spread = jnp.where(lax.div(slot, pair) == block, 1.0, 0.0).astype(jnp.bfloat16)
         limits = jnp.dot(counts, spread, preferred_element_type=jnp.float32)
-        slot_ids = lax.rem(lax.broadcasted_iota(jnp.int32, (V, slots), 1), pair)
-        used = slot_ids.astype(jnp.float32) < limits[:V]
-        total = jnp.where(used, total, 0.0)
-        for t in range(lane_tiles):
-            prod_out[it, t, 0:V, 0:width] = total[:, t * width : (t + 1) * width]
+        slot_ids = lax.rem(lax.broadcasted_iota(jnp.int32, (1, slots), 1), pair)
+        used = slot_ids.astype(jnp.float32) < limits[:1]
+        for i in range(V):
+            total = jnp.where(used, totals[i], 0.0)
+            for t in range(lane_tiles):
+                prod_out[it, t, i : i + 1, 0:width] = total[:, t * width : (t + 1) * width]
         prod_in[it, me] = prod_out[it, lax.div(me * pair, width)]
 
         def send(k, carry):
@@ -227,6 +233,8 @@
             )
             base[v] = fixed[v] - added
 
+    for k in (4, 5, 7):
+        fetches[k].wait()
     send_products(0)
 
     def skew_coup(m, carry):
@@ -237,8 +245,12 @@
         skew(lambda x: inv_ref[m, x], inv, m, 0)
         return carry
 
-    lax.fori_loop(0, 6 * V * V, skew_coup, 0)
-    lax.fori_loop(0, V * V, skew_inv, 0)
+    fetches[3].wait()
+    lax.fori_loop(0, 6 * V * V, skew_coup, 0, unroll=V)
+    fetches[2].wait()
+    lax.fori_loop(0, V * V, skew_inv, 0, unroll=V)
+    fetches[0].wait()
+    fetches[6].wait()
     for v in range(V):
         skew(lambda x: source_ref[v, x], fixed, v, 0)
 
@@ -440,13 +452,25 @@
     padded = rows + 4 * step
     sweeps = 2 * ITERS + 1
     vmem = pl.BlockSpec(memory_space=pltpu.VMEM)
+    operands = (
+        adjoint_source,
+        initial,
+        inverses.reshape(V * V, CX, CY, CZ),
+        couplings.reshape(6 * V * V, CX, CY, CZ),
+        interface_tiles.transpose(1, 2, 0, 3),
+        source_cells,
+        target_cells,
+        tile_counts,
+    )
     f32 = jnp.float32
     return pl.pallas_call(
         functools.partial(kernel, sizes),
         out_shape=jax.ShapeDtypeStruct(initial.shape, f32),
-        in_specs=[vmem] * 8,
+        in_specs=[pl.BlockSpec(memory_space=pltpu.HBM)] * len(operands),
         out_specs=vmem,
         scratch_shapes=[
+            *[pltpu.VMEM(operand.shape, operand.dtype) for operand in operands],
+            pltpu.SemaphoreType.DMA((len(operands),)),
             pltpu.VMEM((6 * V * V, rows, LANES), f32),
             pltpu.VMEM((V * V, rows, LANES), f32),
             pltpu.VMEM((V, padded, LANES), f32),
@@ -468,18 +492,9 @@
             pltpu.SemaphoreType.DMA((ITERS, N)),
         ],
         compiler_params=pltpu.CompilerParams(
-            collective_id=0, has_side_effects=True, vmem_limit_bytes=48 * 1024 * 1024
+            collective_id=0, has_side_effects=True, vmem_limit_bytes=64 * 1024 * 1024
         ),
-    )(
-        adjoint_source,
-        initial,
-        inverses.reshape(V * V, CX, CY, CZ),
-        couplings.reshape(6 * V * V, CX, CY, CZ),
-        interface_tiles,
-        source_cells,
-        target_cells,
-        tile_counts,
-    )
+    )(*operands)
 
 
 def solution(mesh):

time: 114 us -> 108 us (0.947)
  local copies, waits for them, and re-layouts: 8.01 us -> 1.59 us
    unnamed x16 -> x1, local copies, waits for them, and re-layouts: 8.01 us -> 1.59 us
where the time goes in v2:
time: 108 us
  Pallas kernels  107 us (99%)
  local copies, waits for them, and re-layouts  1.59 us (1%)
    pallas_call x1, Pallas kernels, per_device(): pl.pallas_call(functools.partial(kernel, sizes), out_shape=jax.ShapeDtype...  107 us

profile of v2, /device:TPU:0, one launch (start us, length us, event | category | flops | bytes accessed | tf_op | source)
XLA Modules:
  0.0 108.1 jit_solution(5335833386940812528)
XLA Ops:
  0.0 106.5 %shard_map.82 = f32[5,4,4,512]{3,2,1,0:T(4,128)} custom-call(f32[5,4,4,512]{3,2,1,0:T(4,128)} %refs_0_.1, f32[5,4,4,512]{3,2,1,0:T(4,128)} %refs_1_.1, f32[25,4,4,512]{3,2,1,0:T(4,128)} %bitcast.4, bf16[150,4,4,512]{3,2,1,0:T(4,128)(2,1)} %bitcast.3, f32[5,5,1,64]{3,2,1,0:T(1,128)} %bitcast.5, s32[1,64]{1,0:T(1,128)} %refs_5_.1, s32[1,64]{1,0:T(1,128)} %refs_6_.1, ...), custom_call_target="tpu_custom_call" | custom-call | tf_op jit(solution)/shard_map/pallas_call | solution.py:466
  106.5 1.6 %copy.10 = f32[5,4,4,512]{3,2,1,0:T(4,128)} copy(f32[5,4,4,512]{3,2,1,0:T(4,128)} %shard_map.82) | data formatting | bytes 327680

commit v3 on v2

--- a/solution.py
+++ b/solution.py
@@ -192,7 +192,7 @@
             copy_p(it, lax.rem(me + k, N)).start()
             return carry
 
-        lax.fori_loop(1, N, send, 0)
+        lax.fori_loop(1, N, send, 0, unroll=True)
 
     lane_ids = lax.broadcasted_iota(jnp.int32, (8, LANES), 1)
 
@@ -209,7 +209,7 @@
             ).wait_recv()
             return carry
 
-        lax.fori_loop(1, N, wait, 0)
+        lax.fori_loop(1, N, wait, 0, unroll=True)
         mine = lax.rem(me * pair, width)
         own = (lane_ids >= mine) & (lane_ids < mine + pair)
         per_tile = width // pair
@@ -280,6 +280,31 @@
             sums.append(by_x + by_y)
         return sums
 
+    def by_inverse(vector, at, rows):
+        results = []
+        for i in range(V):
+            total = inv[i * V, at : at + rows, :] * vector[0]
+            for j in range(1, V):
+                total += inv[i * V + j, at : at + rows, :] * vector[j]
+            results.append(total)
+        return results
+
+    def precondition(chosen):
+        def chunk(c, carry):
+            at = pl.ds(pl.multiple_of(c * 8, 8), 8)
+            own = [inv[k, at, :] for k in range(V * V)]
+            for m in chosen:
+                for j in range(V):
+                    column = [mats[(m * V + k) * V + j, at, :] for k in range(V)]
+                    for i in range(V):
+                        total = own[i * V] * column[0]
+                        for k in range(1, V):
+                            total += own[i * V + k] * column[k]
+                        mats[(m * V + i) * V + j, at, :] = total
+            return carry
+
+        lax.fori_loop(0, ROWS // 8, chunk, 0)
+
     def make_terms(d):
         at, rows = span(d)
         lane = lax.broadcasted_iota(jnp.int32, (rows, LANES), 1)
@@ -293,14 +318,17 @@
             after = jnp.where(tile == ZT - 1, 0.0, after)
             down.append(pltpu.roll(jnp.where(lane == LANES - 1, before, value), 1, 1))
             up.append(pltpu.roll(jnp.where(lane == 0, after, value), LANES - 1, 1))
+        rest = []
         for i in range(V):
-            total = base[i, at : at + rows, :] - products[i, at : at + rows, :]
             low = mat(4, i, 0, at, rows) * down[0]
             high = mat(5, i, 0, at, rows) * up[0]
             for j in range(1, V):
                 low += mat(4, i, j, at, rows) * down[j]
                 high += mat(5, i, j, at, rows) * up[j]
-            terms[i, at : at + rows, :] = total - (low + high)
+            rest.append(base[i, at : at + rows, :] - (low + high))
+        solved = by_inverse(rest, at, rows)
+        for i in range(V):
+            terms[i, at : at + rows, :] = solved[i] - products[i, at : at + rows, :]
 
     def take_x(s, k, to, at):
         copy_x(s, k, to).wait_recv()
@@ -330,7 +358,7 @@
         m_x, m_y = (0, 2) if forward else (1, 3)
         inflow_x, outflow_x = (has_low_x, has_high_x) if forward else (has_high_x, has_low_x)
         inflow_y, outflow_y = (has_low_y, has_high_y) if forward else (has_high_y, has_low_y)
-        halo, edge_x, edge_y = (-1, CX - 1, CY - 1) if forward else (None, 0, 0)
+        edge_x, edge_y = (CX - 1, CY - 1) if forward else (0, 0)
         halo_x = -1 if forward else CX
         halo_y = -1 if forward else CY
         first_x = 0 if forward else CX - 1
@@ -349,15 +377,9 @@
                 )
             at, rows = span(d)
             sums = side_products(d, m_x, m_y, sign)
-            right = []
             for i in range(V):
+                field[i, PAD + at : PAD + at + rows, :] = terms[i, at : at + rows, :] - sums[i]
                 products[i, at : at + rows, :] = sums[i]
-                right.append(terms[i, at : at + rows, :] - sums[i])
-            for i in range(V):
-                fresh = inv[i * V, at : at + rows, :] * right[0]
-                for j in range(1, V):
-                    fresh += inv[i * V + j, at : at + rows, :] * right[j]
-                field[i, PAD + at : PAD + at + rows, :] = fresh
             y = d - edge_x
             if 0 <= y < CY:
                 pl.when(outflow_x)(
@@ -381,9 +403,16 @@
 
     for d in range(DIAGS):
         at, rows = span(d)
-        sums = side_products(d, 1, 3, 1)
+        sums = by_inverse(side_products(d, 1, 3, 1), at, rows)
         for i in range(V):
             products[i, at : at + rows, :] = sums[i]
+
+    early = p + q < (NP + NQ) // 3
+    precondition((0, 2))
+
+    @pl.when(jnp.logical_not(early))
+    def _():
+        precondition((1, 3))
 
     def iteration(it, carry):
         @pl.when(it > 0)
@@ -394,6 +423,11 @@
         for d in range(DIAGS):
             make_terms(d)
         sweep(2 * it + 1, True)
+
+        @pl.when((it == 0) & early)
+        def _():
+            precondition((1, 3))
+
         for d in range(DIAGS):
             make_terms(d)
         sweep(2 * it + 2, False)

time: 108 us -> 108 us (level)
  no operation moved by 1% of the time
where the time goes in v3:
time: 108 us
  Pallas kernels  106 us (98%)
  local copies, waits for them, and re-layouts  1.59 us (1%)
    pallas_call x1, Pallas kernels, per_device(): pl.pallas_call(functools.partial(kernel, sizes), out_shape=jax.ShapeDtype...  106 us

profile of v3, /device:TPU:0, one launch (start us, length us, event | category | flops | bytes accessed | tf_op | source)
XLA Modules:
  0.0 107.6 jit_solution(263373425238469220)
XLA Ops:
  0.0 106.0 %shard_map.82 = f32[5,4,4,512]{3,2,1,0:T(4,128)} custom-call(f32[5,4,4,512]{3,2,1,0:T(4,128)} %refs_0_.1, f32[5,4,4,512]{3,2,1,0:T(4,128)} %refs_1_.1, f32[25,4,4,512]{3,2,1,0:T(4,128)} %bitcast.4, bf16[150,4,4,512]{3,2,1,0:T(4,128)(2,1)} %bitcast.3, f32[5,5,1,64]{3,2,1,0:T(1,128)} %bitcast.5, s32[1,64]{1,0:T(1,128)} %refs_5_.1, s32[1,64]{1,0:T(1,128)} %refs_6_.1, ...), custom_call_target="tpu_custom_call" | custom-call | tf_op jit(solution)/shard_map/pallas_call | solution.py:500
  106.0 1.6 %copy.10 = f32[5,4,4,512]{3,2,1,0:T(4,128)} copy(f32[5,4,4,512]{3,2,1,0:T(4,128)} %shard_map.82) | data formatting | bytes 327680
